TPU v7x, 256 devices: a whole 4x4x8 slice. The times are simulated.
256 devices in a mesh: grid: 32 (over y_hi, z, core), chan: 8 (over x, y_lo).
Axes of the slice: x: 4, y: 4 (y_hi: 2, y_lo: 2; y = y_hi * 2 + y_lo), z: 8, core: 2. Of those that a mesh axis runs over, the one named last changes fastest.
Arguments:
- activations: bfloat16 [256, 32, 8, 16, 128], P('chan', 'grid'), may hold values from -6 to 6
- grad_out: bfloat16 [256, 32, 16, 128], P('chan', 'grid'), may hold values from -6 to 6
- weight: bfloat16 [27, 256, 256], P(None, 'chan'), may hold values from -0.078125 to 0.078125
Outputs:
- grad_act: bfloat16 [256, 32, 8, 16, 128], P('chan', 'grid')
- grad_weight: float32 [27, 256, 256], P(None, 'chan')
All inputs are finite; a program needn't handle non-finite values.
Results may differ from a plain program's by a relative error of at most 0.001.
Values may be sent and summed in bfloat16 or wider, within the bound.
A program may use at most 64 MiB of HBM per device.

v0:
```python
import math
import jax
import jax.numpy as jnp
from jax import lax
from jax.sharding import PartitionSpec as P


def shifted_2(block, axis, distance):
    devices = range(lax.axis_size(axis))
    route = [(i - distance, i) for i in devices if i - distance in devices]
    return lax.ppermute(block, axis, route)


def parity_taps(parity):
    if parity == 0:
        return [(1, 0)]
    return [(2, 0), (0, 1)]


def tap_parity(tap):
    if tap == 1:
        return (0, 0)
    if tap == 2:
        return (1, 0)
    return (1, 1)


def shifted_grads(grad_cells, rim_plane):
    result = {}
    for step_x in range(2):
        if step_x == 0:
            x_shifted = grad_cells
        else:
            x_shifted = jnp.concatenate([grad_cells[:, 1:], rim_plane[:, None]], 1)
        for step_y in range(2):
            if step_y == 0:
                y_shifted = x_shifted
            else:
                y_shifted = jnp.concatenate(
                    [x_shifted[:, :, 1:], jnp.zeros_like(x_shifted[:, :, :1])], 2
                )
            for step_z in range(2):
                if step_z == 0:
                    z_shifted = y_shifted
                else:
                    z_shifted = jnp.concatenate(
                        [y_shifted[:, :, :, 1:], jnp.zeros_like(y_shifted[:, :, :, :1])], 3
                    )
                result[step_x, step_y, step_z] = z_shifted
    return result


def on_device(activations, grad_out, weight):
    cin_dev, planes, parities, out_y, out_z = activations.shape
    count_out = planes * out_y * out_z
    scale_norm = 1.0 / math.sqrt(count_out * lax.axis_size("grid"))
    front_plane = shifted_2(activations[:, planes - 1 : planes, 4:8], "grid", 1)
    act_before = jnp.concatenate([front_plane, activations[:, : planes - 1, 4:8]], 1)
    gathered = lax.all_gather(grad_out, "chan", axis=0, tiled=True)
    rim_whole = shifted_2(gathered[:, 0], "grid", -1)
    piece_rows = gathered.shape[0]
    shifted = shifted_grads(gathered, rim_whole)
    blocks = []
    for parity in range(8):
        par_x, par_y, par_z = (parity // 4, parity // 2 % 2, parity % 2)
        block_sum = jnp.zeros((cin_dev, count_out), jnp.float32)
        for tap_x, step_x in parity_taps(par_x):
            for tap_y, step_y in parity_taps(par_y):
                for tap_z, step_z in parity_taps(par_z):
                    window = shifted[step_x, step_y, step_z].reshape(piece_rows, count_out)
                    block_sum = block_sum + jnp.dot(
                        weight[tap_x * 9 + tap_y * 3 + tap_z],
                        window,
                        preferred_element_type=jnp.float32,
                    )
        blocks.append(block_sum.reshape(cin_dev, planes, out_y, out_z))
    totals = jnp.stack(blocks, 2)
    tap_list = []
    for tap_index in range(27):
        tap_x = tap_index // 9
        par_x, step_x = tap_parity(tap_x)
        par_y, step_y = tap_parity(tap_index // 3 % 3)
        par_z, step_z = tap_parity(tap_index % 3)
        par_index = 4 * par_x + 2 * par_y + par_z
        if tap_x == 0:
            act_slab = act_before[:, :, par_index - 4]
            grad_slab = shifted[0, step_y, step_z]
        else:
            act_slab = activations[:, :, par_index]
            grad_slab = shifted[step_x, step_y, step_z]
        tap_list.append(
            jnp.einsum("cxyz,oxyz->co", act_slab, grad_slab, preferred_element_type=jnp.float32)
        )
    tap_terms = jnp.stack(tap_list, 0)
    grad_w = tap_terms
    totals, grad_w = (totals, grad_w)
    grad_act = totals.astype(jnp.bfloat16)
    grad_weight = lax.psum(grad_w, "grid") * scale_norm
    return (grad_act, grad_weight)


def solution(mesh):
    placed = (
        P("chan", "grid", None, None, None),
        P("chan", "grid", None, None),
        P(None, "chan", None),
    )
    return jax.shard_map(
        on_device,
        mesh=mesh,
        in_specs=placed,
        out_specs=(P("chan", "grid", None, None, None), P(None, "chan", None)),
        check_vma=False,
    )
```

profile of v0, /device:TPU:1, one launch (start us, length us, event | category | flops | bytes accessed | tf_op | source)
XLA Modules:
  0.0 415.9 jit_solution(3259047934980850593)
XLA Ops:
  11.0 4.9 %collective-permute-start.1 = (bf16[32,1,4,16,128]{4,0,3,2,1:T(8,128)(2,1)}, bf16[32,1,4,16,128]{4,0,3,2,1:T(8,128)(2,1)}, u32[]{:S(2)}, u32[]{:S(2)}) collective-permute-start(bf16[32,1,4,16,128]{4,0,3,2,1:T(8,128)(2,1)} %copy.42), channel_id=1, source_target_pairs={{0,8},{8,16},{16,24},{24,32},{32,40},{40,48},{48,56},{56,64},{64,7... | collective-permute-start | bytes 1572872 | tf_op jit(solution)/shard_map/ppermute | solution.py:11
  16.9 34.0 %all-gather.2.cloned.1.call-done = bf16[256,1,16,128]{3,0,2,1:T(8,128)(2,1)} async-done(((bf16[32,1,16,128]{3,0,2,1:T(8,128)(2,1)}), bf16[256,1,16,128]{3,0,2,1:T(8,128)(2,1)}) %all-gather.2.cloned.1.call-update) | async-done | bytes 1048592 | tf_op jit(solution)/shard_map/all_gather | solution.py:59
  52.4 1.8 fusion.23
  54.2 1.8 fusion.105
  56.1 1.8 fusion.102
  57.9 1.9 fusion.99
  59.8 1.8 fusion.91
  65.7 2.4 copy.93
  68.1 2.4 copy.95
  70.5 1.9 fusion.86
  72.4 1.8 fusion.81
  74.2 1.9 fusion.57
  76.1 2.0 fusion.56
  78.2 1.9 fusion.55
  80.1 1.9 fusion.54
  82.0 1.9 fusion.53
  84.0 1.9 fusion.52
  85.9 1.9 fusion.51
  87.8 1.9 fusion.50
  89.8 1.9 fusion.49
  119.3 7.8 %collective-permute-start = (bf16[256,16,128]{2,0,1:T(8,128)(2,1)S(1)}, bf16[256,16,128]{2,0,1:T(8,128)(2,1)S(1)}, u32[]{:S(2)}, u32[]{:S(2)}) collective-permute-start(bf16[256,16,128]{2,0,1:T(8,128)(2,1)S(1)} %bitcast.519), channel_id=1, source_target_pairs={{8,0},{16,8},{24,16},{32,24},{40,32},{48,40},{56,48},{64,56},{72,6... | collective-permute-start | bytes 3145736 | tf_op jit(solution)/shard_map/ppermute | solution.py:11
  127.2 1.8 fusion.9
  133.4 1.8 fusion.94
  136.4 1.9 fusion.3
  138.2 237.4 %all-reduce.8.cloned.1.call-done = f32[27,32,256]{2,1,0:T(8,128)} async-done(((f32[27,32,256]{2,1,0:T(8,128)}), f32[27,32,256]{2,1,0:T(8,128)}) %all-reduce.8.cloned.1.call-update) | async-done | bytes 884752 | tf_op jit(solution)/shard_map/psum | solution.py:98
  375.6 2.2 broadcast_multiply_fusion
  381.8 1.8 convolution_bitcast_fusion.6
  383.7 1.8 convolution_bitcast_fusion.1
  385.5 2.4 copy.51
  389.2 1.8 convolution_bitcast_fusion.8
  391.0 1.8 convolution_bitcast_fusion.2
  406.5 2.6 copy.41
  (123 shorter events, 62.1 us)
Async XLA Ops:
  7.2 43.8 %all-gather.2.cloned.1.call-start = ((), (), s32[]{:S(2)}) async-start(), calls=%async_computation | async-start | bytes 1179648 | tf_op jit(solution)/shard_map/all_gather | solution.py:59
  8.8 1.0 slice-start
  8.8 7.1 %copy-start.6 = (bf16[32,1,8,16,128]{4,3,2,1,0:T(8,128)(2,1)S(1)}, bf16[32,1,8,16,128]{4,3,2,1,0:T(8,128)(2,1)}, u32[]{:S(2)}) copy-start(bf16[32,1,8,16,128]{4,3,2,1,0:T(8,128)(2,1)} %param.3) | copy-start | bytes 3145732
  8.9 366.8 %all-reduce.8.cloned.1.call-start = ((), (), s32[]{:S(2)}) async-start(), calls=%async_computation.1 | async-start | bytes 1769472 | tf_op jit(solution)/shard_map/psum | solution.py:98
  11.0 63.2 %collective-permute-start.1 = (bf16[32,1,4,16,128]{4,0,3,2,1:T(8,128)(2,1)}, bf16[32,1,4,16,128]{4,0,3,2,1:T(8,128)(2,1)}, u32[]{:S(2)}, u32[]{:S(2)}) collective-permute-start(bf16[32,1,4,16,128]{4,0,3,2,1:T(8,128)(2,1)} %copy.42), channel_id=1, source_target_pairs={{0,8},{8,16},{16,24},{24,32},{32,40},{40,48},{48,56},{56,64},{64,7... | collective-permute-start | bytes 1572872 | tf_op jit(solution)/shard_map/ppermute | solution.py:11
  57.9 3.8 copy-start
  70.4 3.8 copy-start.2
  76.1 4.0 copy-start.1
  91.7 1.0 copy-start.8
  93.8 1.0 copy-start.9
  94.8 1.0 copy-start.23
  103.1 1.0 copy-start.7
  104.1 1.0 copy-start.22
  109.3 1.2 copy-start.4
  110.5 0.9 copy-start.16
  110.6 2.0 copy-start.5
  112.6 1.0 copy-start.15
  114.7 1.0 copy-start.13
  116.8 1.3 copy-start.3
  119.3 7.9 %copy-start.10 = (f32[32,2048]{1,0:T(8,128)S(1)}, f32[32,2048]{1,0:T(8,128)}, u32[]{:S(2)}) copy-start(f32[32,2048]{1,0:T(8,128)} %fusion.91) | copy-start | bytes 786436
  119.3 9.7 %copy-start.12 = (f32[32,2048]{1,0:T(8,128)S(1)}, f32[32,2048]{1,0:T(8,128)}, u32[]{:S(2)}) copy-start(f32[32,2048]{1,0:T(8,128)} %fusion.86) | copy-start | bytes 786436
  119.3 258.4 %collective-permute-start = (bf16[256,16,128]{2,0,1:T(8,128)(2,1)S(1)}, bf16[256,16,128]{2,0,1:T(8,128)(2,1)S(1)}, u32[]{:S(2)}, u32[]{:S(2)}) collective-permute-start(bf16[256,16,128]{2,0,1:T(8,128)(2,1)S(1)} %bitcast.519), channel_id=1, source_target_pairs={{8,0},{16,8},{24,16},{32,24},{40,32},{48,40},{56,48},{64,56},{72,6... | collective-permute-start | bytes 3145736 | tf_op jit(solution)/shard_map/ppermute | solution.py:11
  129.0 1.2 copy-start.11
  393.7 1.5 copy-start.19
  395.2 1.0 copy-start.14
  397.3 1.0 copy-start.18
  400.1 1.0 copy-start.17
  400.1 1.0 copy-start.20
  400.1 1.1 copy-start.21
  403.5 0.9 copy-start.24
Sparse Core Ops, SparseCore 0:
  10.4 40.5 all-gather.1
  110.5 265.1 all-reduce.7
where the time goes:
time: 419 us; the launch traced here: 416 us
  waiting for transfers between devices  271 us (65%)
  matrix products  77 us (18%)
  local copies, waits for them, and re-layouts  38 us (9%)
  between operations  14.5 us (3%)
  starting transfers between devices  12.8 us (3%)
    psum x1, waiting for transfers between devices, on_device(): grad_weight = lax.psum(grad_w, 'grid') * scale_norm  237 us
    dot_general x27, matrix products, on_device(): jnp.dot(weight[tap_x * 9 + tap_y * 3 + tap_z], window, preferred_element_...  40.9 us
    dot_general x27, matrix products, on_device(): jnp.einsum('cxyz,oxyz->co', act_slab, grad_slab, preferred_element_type=j...  36.1 us
    all_gather x1, waiting for transfers between devices, on_device(): gathered = lax.all_gather(grad_out, 'chan', axis=0, tiled=True)  34 us
    unnamed x72, local copies, waits for them, and re-layouts  25.9 us
    ppermute x2, starting transfers between devices, shifted_2(): return lax.ppermute(block, axis, route)  12.7 us
  transfers between devices with their start and end apart: 4, of which 2 were waited for; matrix products, arithmetic and copies ran while one was open for 11% of the time, Pallas kernels for 0%

commit v1 on v0

--- a/solution.py
+++ b/solution.py
@@ -95,7 +95,7 @@
     grad_w = tap_terms
     totals, grad_w = (totals, grad_w)
     grad_act = totals.astype(jnp.bfloat16)
-    grad_weight = lax.psum(grad_w, "grid") * scale_norm
+    grad_weight = jnp.sum(lax.all_gather(grad_w, "grid"), axis=0) * scale_norm
     return (grad_act, grad_weight)
 
 

time: 419 us -> 332 us (0.79)
  waiting for transfers between devices: 271 us -> 171 us
  other arithmetic: 2.17 us -> 11.2 us
    psum x1 -> x0, waiting for transfers between devices: 237 us -> none  [on_device(): grad_weight = lax.psum(grad_w, 'grid') * scale_norm]
    all_gather x0 -> x1, waiting for transfers between devices: none -> 120 us  [on_device(): grad_weight = jnp.sum(lax.all_gather(grad_w, 'grid'), axis=0) * scale_norm]
    ppermute x2, waiting for transfers between devices: 0.01 us -> 19.1 us  [shifted_2(): return lax.ppermute(block, axis, route)]
    reduce_sum x0 -> x1, other arithmetic: none -> 10.2 us  [on_device(): grad_weight = jnp.sum(lax.all_gather(grad_w, 'grid'), axis=0) * scale_norm]
    dot_general x27, matrix products: 36.1 us -> 44.7 us  [on_device(): jnp.einsum('cxyz,oxyz->co', act_slab, grad_slab, preferred_element_type=j...]
    dot_general x27, matrix products: 40.9 us -> 33.6 us  [on_device(): jnp.dot(weight[tap_x * 9 + tap_y * 3 + tap_z], window, preferred_element_...]
    unnamed x72 -> x36, local copies, waits for them, and re-layouts: 25.9 us -> 20.3 us
  transfers between devices with their start and end apart: 4 -> 4, of which waited for: 2 -> 3; matrix products, arithmetic and copies ran while one was open for 11% -> 22% of each run, Pallas kernels for 0% -> 0%
where the time goes in v1:
time: 332 us; the launch traced here: 329 us
  waiting for transfers between devices  171 us (52%)
  matrix products  78.2 us (24%)
  local copies, waits for them, and re-layouts  40.9 us (12%)
  between operations  14.3 us (4%)
  starting transfers between devices  12.8 us (4%)
  other arithmetic  11.2 us (3%)
    all_gather x1, waiting for transfers between devices, on_device(): grad_weight = jnp.sum(lax.all_gather(grad_w, 'grid'), axis=0) * scale_norm  120 us
    dot_general x27, matrix products, on_device(): jnp.einsum('cxyz,oxyz->co', act_slab, grad_slab, preferred_element_type=j...  44.7 us
    dot_general x27, matrix products, on_device(): jnp.dot(weight[tap_x * 9 + tap_y * 3 + tap_z], window, preferred_element_...  33.6 us
    all_gather x1, waiting for transfers between devices, on_device(): gathered = lax.all_gather(grad_out, 'chan', axis=0, tiled=True)  32.8 us
    unnamed x36, local copies, waits for them, and re-layouts  20.3 us
    ppermute x2, waiting for transfers between devices, shifted_2(): return lax.ppermute(block, axis, route)  19.1 us
    ppermute x2, starting transfers between devices, shifted_2(): return lax.ppermute(block, axis, route)  12.7 us
    reduce_sum x1, other arithmetic, on_device(): grad_weight = jnp.sum(lax.all_gather(grad_w, 'grid'), axis=0) * scale_norm  10.2 us
  transfers between devices with their start and end apart: 4, of which 3 were waited for; matrix products, arithmetic and copies ran while one was open for 22% of the time, Pallas kernels for 0%

profile of v1, /device:TPU:1, one launch (start us, length us, event | category | flops | bytes accessed | tf_op | source)
XLA Modules:
  0.0 328.9 jit_solution(13872411936002487124)
XLA Ops:
  11.1 4.9 %collective-permute-start.1 = (bf16[32,1,4,16,128]{4,0,3,2,1:T(8,128)(2,1)}, bf16[32,1,4,16,128]{4,0,3,2,1:T(8,128)(2,1)}, u32[]{:S(2)}, u32[]{:S(2)}) collective-permute-start(bf16[32,1,4,16,128]{4,0,3,2,1:T(8,128)(2,1)} %copy.68), channel_id=1, source_target_pairs={{0,8},{8,16},{16,24},{24,32},{32,40},{40,48},{48,56},{56,64},{64,7... | collective-permute-start | bytes 1572872 | tf_op jit(solution)/shard_map/ppermute | solution.py:11
  16.0 2.2 fusion.162
  18.3 32.8 %all-gather.4.cloned.1.call-done = bf16[256,1,16,128]{3,0,2,1:T(8,128)(2,1)} async-done(((bf16[32,1,16,128]{3,0,2,1:T(8,128)(2,1)}), bf16[256,1,16,128]{3,0,2,1:T(8,128)(2,1)}) %all-gather.4.cloned.1.call-update) | async-done | bytes 1048592 | tf_op jit(solution)/shard_map/all_gather | solution.py:59
  51.0 1.7 slice.199
  54.4 2.1 fusion.57
  56.5 1.9 fusion.56
  58.4 1.9 fusion.55
  60.3 1.9 fusion.54
  62.3 2.3 fusion.53
  64.6 2.3 fusion.52
  66.9 1.9 fusion.51
  68.9 2.3 fusion.50
  71.2 2.3 fusion.49
  74.6 1.9 fusion.47
  77.5 1.9 fusion.45
  79.5 2.3 fusion.44
  81.8 2.3 fusion.43
  85.2 2.3 fusion.41
  87.5 2.3 fusion.40
  101.8 2.4 copy.121
  117.9 7.8 %collective-permute-start = (bf16[256,16,128]{2,0,1:T(8,128)(2,1)S(1)}, bf16[256,16,128]{2,0,1:T(8,128)(2,1)S(1)}, u32[]{:S(2)}, u32[]{:S(2)}) collective-permute-start(bf16[256,16,128]{2,0,1:T(8,128)(2,1)S(1)} %bitcast.520), channel_id=1, source_target_pairs={{8,0},{16,8},{24,16},{32,24},{40,32},{48,40},{56,48},{64,56},{72,6... | collective-permute-start | bytes 3145736 | tf_op jit(solution)/shard_map/ppermute | solution.py:11
  126.9 1.9 fusion.94
  131.1 1.9 fusion.9
  137.5 1.8 fusion.3
  139.3 19.1 %collective-permute-done = bf16[256,16,128]{2,0,1:T(8,128)(2,1)S(1)} collective-permute-done((bf16[256,16,128]{2,0,1:T(8,128)(2,1)S(1)}, bf16[256,16,128]{2,0,1:T(8,128)(2,1)S(1)}, u32[]{:S(2)}, u32[]{:S(2)}) %collective-permute-start) | collective-permute-done | bytes 1048608 | tf_op jit(solution)/shard_map/ppermute | solution.py:11
  159.5 1.8 copy.47
  173.6 2.5 pad_slice_fusion
  176.1 2.6 copy.78
  185.7 1.6 copy_dynamic-update-slice_fusion.2
  188.7 2.6 copy.67
  191.3 119.5 %all-gather.6.cloned.1.call-done = f32[864,32,256]{2,1,0:T(8,128)} async-done(((f32[27,32,256]{2,1,0:T(8,128)}), f32[864,32,256]{2,1,0:T(8,128)}) %all-gather.6.cloned.1.call-update) | async-done | bytes 28311568 | tf_op jit(solution)/shard_map/all_gather | solution.py:98
  310.8 10.2 %reduce_sum.9 = f32[27,32,256]{2,1,0:T(8,128)S(1)} reduce(f32[32,27,32,256]{3,2,1,0:T(8,128)} %bitcast.528, f32[]{:T(128)} %constant.0.clone.1), dimensions={0}, to_apply=%region_0.0 | reduce | flops 6856704 | bytes 29196292 | tf_op jit(solution)/shard_map/reduce_sum | solution.py:98
  (87 shorter events, 64.9 us)
Async XLA Ops:
  7.2 43.9 %all-gather.4.cloned.1.call-start = ((), (), s32[]{:S(2)}) async-start(), calls=%async_computation | async-start | bytes 1179648 | tf_op jit(solution)/shard_map/all_gather | solution.py:59
  8.8 302.0 %all-gather.6.cloned.1.call-start = ((), (), s32[]{:S(2)}) async-start(), calls=%async_computation.1 | async-start | bytes 29196288 | tf_op jit(solution)/shard_map/all_gather | solution.py:98
  11.1 43.2 %collective-permute-start.1 = (bf16[32,1,4,16,128]{4,0,3,2,1:T(8,128)(2,1)}, bf16[32,1,4,16,128]{4,0,3,2,1:T(8,128)(2,1)}, u32[]{:S(2)}, u32[]{:S(2)}) collective-permute-start(bf16[32,1,4,16,128]{4,0,3,2,1:T(8,128)(2,1)} %copy.68), channel_id=1, source_target_pairs={{0,8},{8,16},{16,24},{24,32},{32,40},{40,48},{48,56},{56,64},{64,7... | collective-permute-start | bytes 1572872 | tf_op jit(solution)/shard_map/ppermute | solution.py:11
  51.0 41.8 %copy-start.5 = (bf16[32,1,1,16,128]{4,3,2,1,0:T(8,128)(2,1)S(1)}, bf16[32,1,1,16,128]{4,3,2,1,0:T(8,128)(2,1)}, u32[]{:S(2)}) copy-start(bf16[32,1,1,16,128]{4,3,2,1,0:T(8,128)(2,1)} %get-tuple-element.9) | copy-start | bytes 393220
  51.0 42.9 %copy-start = (bf16[256,1,16,128]{3,0,2,1:T(8,128)(2,1)S(1)}, bf16[256,1,16,128]{3,0,2,1:T(8,128)(2,1)}, u32[]{:S(2)}) copy-start(bf16[256,1,16,128]{3,0,2,1:T(8,128)(2,1)} %all-gather.4.cloned.1.call-done) | copy-start | bytes 3145732
  51.0 42.9 %copy-start.6 = (bf16[32,1,1,16,128]{4,3,2,1,0:T(8,128)(2,1)S(1)}, bf16[32,1,1,16,128]{4,3,2,1,0:T(8,128)(2,1)}, u32[]{:S(2)}) copy-start(bf16[32,1,1,16,128]{4,3,2,1,0:T(8,128)(2,1)} %get-tuple-element.8) | copy-start | bytes 393220
  54.3 35.4 %copy-start.1 = (bf16[256,1,16,127]{3,0,2,1:T(8,128)(2,1)}, bf16[256,1,16,127]{3,0,2,1:T(8,128)(2,1)S(1)}, u32[]{:S(2)}) copy-start(bf16[256,1,16,127]{3,0,2,1:T(8,128)(2,1)S(1)} %pad_slice_fusion.1) | copy-start | bytes 3121156
  117.9 40.6 %collective-permute-start = (bf16[256,16,128]{2,0,1:T(8,128)(2,1)S(1)}, bf16[256,16,128]{2,0,1:T(8,128)(2,1)S(1)}, u32[]{:S(2)}, u32[]{:S(2)}) collective-permute-start(bf16[256,16,128]{2,0,1:T(8,128)(2,1)S(1)} %bitcast.520), channel_id=1, source_target_pairs={{8,0},{16,8},{24,16},{32,24},{40,32},{48,40},{56,48},{64,56},{72,6... | collective-permute-start | bytes 3145736 | tf_op jit(solution)/shard_map/ppermute | solution.py:11
  126.9 31.5 %copy-start.4 = (bf16[32,1,8,16,128]{4,0,3,2,1:T(8,128)(2,1)}, bf16[32,1,8,16,128]{4,0,3,2,1:T(8,128)(2,1)S(1)}, u32[]{:S(2)}) copy-start(bf16[32,1,8,16,128]{4,0,3,2,1:T(8,128)(2,1)S(1)} %copy_dynamic-update-slice_fusion.4) | copy-start | bytes 3145732
  158.4 1.0 copy-start.2
  159.5 9.2 %copy-start.3 = (bf16[256,1,15,128]{3,0,2,1:T(8,128)(2,1)}, bf16[256,1,15,128]{3,0,2,1:T(8,128)(2,1)S(1)}, u32[]{:S(2)}) copy-start(bf16[256,1,15,128]{3,0,2,1:T(8,128)(2,1)S(1)} %slice.202) | copy-start | bytes 2949124
Sparse Core Ops, SparseCore 0:
  10.4 40.6 all-gather.3
  99.2 211.5 all-gather.5
